TPU v7x, 512 devices: a whole 4x4x16 slice. The times are simulated.
512 devices in a mesh: rep: 16 (over z_hi, x, core), exp: 32 (over y, z_lo).
Axes of the slice: x: 4, y: 4, z: 16 (z_hi: 2, z_lo: 8; z = z_hi * 8 + z_lo), core: 2. Of those that a mesh axis runs over, the one named last changes fastest.
Arguments:
- tokens: bfloat16 [65536, 2048], P(('rep', 'exp')), may hold values from -6 to 6
- routes: int32 [65536, 2], P(('rep', 'exp')), may hold values from 0 to 31, all different within a row; in each aligned block of 128 rows (0 to 127, 128 to 255, ...) at most 12 rows name the same one
- route_weight: float32 [65536, 2], P(('rep', 'exp')), may hold values from 0.2 to 1
- gate_up_store: bfloat16 [32, 2048, 1536], P('exp', 'rep'), may hold values from -0.125 to 0.125
- down_store: bfloat16 [32, 768, 2048], P('exp', None, 'rep'), may hold values from -0.21875 to 0.21875
- held_bucket: int32 [16], replicated, may hold values from 0 to 15, each once
Outputs:
- mixed: bfloat16 [65536, 2048], P(('rep', 'exp'))
Inputs may be any that keep to these rules, and one draw needn't show every extreme that they name: `routes`: each token names 2 different experts; within the tokens of one device (aligned blocks of 128 tokens) no expert is named more than 12 times, a bound that some block reaches. `held_bucket`: every bucket is owned by exactly one replica index.
All inputs are finite; a program needn't handle non-finite values.
Results may differ from a plain program's by a relative error of at most 0.0057.
Values may be sent and summed in bfloat16 or wider, within the bound.
A program may use at most 64 MiB of HBM per device.

v0:
```python
import jax
import jax.numpy as jnp
from jax import lax
from jax.sharding import PartitionSpec as P


def reorder_buckets(array_in, bucket_order, bucket_count):
    full_shape = array_in.shape
    blocked = array_in.reshape(full_shape[:-1] + (bucket_count, full_shape[-1] // bucket_count))
    return jnp.take(blocked, bucket_order, axis=len(full_shape) - 1).reshape(full_shape)


def local(tokens, routes, route_weight, gate_up_store, down_store, held_bucket):
    n_exp = lax.axis_size("exp")
    n_rep = lax.axis_size("rep")
    tok_rows, model_width = tokens.shape
    route_count = routes.shape[1]
    local_experts, bucket_rows, double_hidden = gate_up_store.shape
    hidden_units = double_hidden // 2
    experts = n_exp * local_experts
    capacity = 3 * tok_rows * route_count // (2 * experts)
    inverse = jnp.zeros((n_rep,), jnp.int32).at[held_bucket].set(jnp.arange(n_rep, dtype=jnp.int32))
    flat_routes = routes.reshape(-1)
    onehot = (flat_routes[:, None] == jnp.arange(experts, dtype=jnp.int32)[None, :]).astype(
        jnp.int32
    )
    slot_rank = jnp.sum(
        (jnp.cumsum(onehot, axis=0, dtype=jnp.int32) - onehot) * onehot, axis=1, dtype=jnp.int32
    )
    source_rows = jnp.repeat(tokens, route_count, axis=0)
    outgoing = (
        jnp.zeros((experts, capacity, model_width), jnp.bfloat16)
        .at[flat_routes, slot_rank]
        .set(source_rows)
    )
    gate_up_all, down_all = (
        lax.all_gather(gate_up_store, "rep", axis=1, tiled=True),
        lax.all_gather(down_store, "rep", axis=2, tiled=True),
    )
    received = lax.all_to_all(outgoing, "exp", split_axis=0, concat_axis=0, tiled=True)
    slot_count = received.shape[1]
    features = received.reshape(n_exp, local_experts, slot_count, model_width)
    features = reorder_buckets(features, held_bucket, n_rep)
    pre_act = jnp.einsum(
        "secd,edf->secf", features, gate_up_all, preferred_element_type=jnp.float32
    )
    hidden = (jax.nn.silu(pre_act[..., :hidden_units]) * pre_act[..., hidden_units:]).astype(
        jnp.bfloat16
    )
    produced = jnp.einsum(
        "sech,ehd->secd", hidden, down_all, preferred_element_type=jnp.float32
    ).astype(jnp.bfloat16)
    produced = reorder_buckets(produced, inverse, n_rep)
    returned = lax.all_to_all(
        produced.reshape(experts, slot_count, model_width),
        "exp",
        split_axis=0,
        concat_axis=0,
        tiled=True,
    )
    picked = (
        returned[flat_routes, slot_rank]
        .astype(jnp.float32)
        .reshape(tok_rows, route_count, model_width)
    )
    mixed_out = jnp.sum(route_weight[:, :, None] * picked, axis=1)
    return mixed_out.astype(jnp.bfloat16)


def solution(mesh):
    in_specs = (
        P(("rep", "exp"), None),
        P(("rep", "exp"), None),
        P(("rep", "exp"), None),
        P("exp", "rep", None),
        P("exp", None, "rep"),
        P(),
    )
    out_specs = P(("rep", "exp"), None)
    return jax.shard_map(local, mesh=mesh, in_specs=in_specs, out_specs=out_specs, check_vma=False)
```

profile of v0, /device:TPU:32, one launch (start us, length us, event | category | flops | bytes accessed | tf_op | source)
XLA Modules:
  0.0 451.5 jit_solution(4604183296325775035)
XLA Ops:
  7.3 0.8 copy.36
  9.3 1.7 broadcast_in_dim.25
  11.7 22.3 %scatter_fusion = bf16[32,12,2048]{2,0,1:T(8,128)(2,1)S(1)} fusion(bf16[32,12,2048]{2,0,1:T(8,128)(2,1)S(1)} %broadcast_in_dim.24, s32[256]{0:T(256)S(1)} %bitcast.79, bf16[256,2048]{1,0:T(8,128)(2,1)S(1)} %reshape.139), kind=kCustom, calls=%fused_computation.3 | custom fusion | bytes 3147776 | tf_op jit(solution)/shard_map/scatter | solution.py:34
  34.1 2.3 copy.40
  36.4 15.6 %all-to-all-start = ((bf16[32,12,2048]{2,1,0:T(8,128)(2,1)}), bf16[32,12,2048]{2,1,0:T(8,128)(2,1)}, u32[]{:S(2)}, u32[]{:S(2)}) async-start(bf16[32,12,2048]{2,1,0:T(8,128)(2,1)} %copy.40), calls=%async_computation | async-start | bytes 4194304 | tf_op jit(solution)/shard_map/all_to_all | solution.py:40
  52.8 0.8 scatter_custom_fusion.1
  53.7 162.3 %all-to-all-done = bf16[32,12,2048]{2,1,0:T(8,128)(2,1)} async-done(((bf16[32,12,2048]{2,1,0:T(8,128)(2,1)}), bf16[32,12,2048]{2,1,0:T(8,128)(2,1)}, u32[]{:S(2)}, u32[]{:S(2)}) %all-to-all-start) | async-done | bytes 1572896 | tf_op jit(solution)/shard_map/all_to_all | solution.py:40
  216.0 3.0 reshape.164
  219.0 1.0 copy.58
  220.0 0.9 gather_fusion.1
  221.1 1.0 copy.43
  222.1 0.7 reshape.105
  222.9 6.8 %fusion.4 = f32[32,1,12,1536]{3,0,2,1:T(8,128)} fusion(bf16[32,12,2048]{2,0,1:T(8,128)(2,1)S(1)} %reshape.105, bf16[1,2048,1536]{2,1,0:T(8,128)(2,1)} %all-gather.3.cloned.1.call-done), kind=kOutput, calls=%fused_computation.9 | convolution fusion | flops 2415919104 | bytes 10223616 | tf_op jit(solution)/shard_map/secd,edf->secf/dot_general | solution.py:44
  229.7 83.4 %all-gather.5.cloned.1.call-done = bf16[1,768,2048]{2,1,0:T(8,128)(2,1)} async-done(((bf16[1,768,128]{2,1,0:T(8,128)(2,1)}), bf16[1,768,2048]{2,1,0:T(8,128)(2,1)}) %all-gather.5.cloned.1.call-update) | async-done | bytes 3145744 | tf_op jit(solution)/shard_map/all_gather | solution.py:38
  313.1 4.0 fusion.10
  317.4 0.9 gather_fusion.2
  318.5 1.0 copy.50
  319.5 2.0 reshape.165
  321.5 14.1 %all-to-all-start.1 = ((bf16[32,12,2048]{2,1,0:T(8,128)(2,1)}), bf16[32,12,2048]{2,1,0:T(8,128)(2,1)}, u32[]{:S(2)}, u32[]{:S(2)}) async-start(bf16[32,12,2048]{2,1,0:T(8,128)(2,1)} %reshape.165), calls=%async_computation.1 | async-start | bytes 4194304 | tf_op jit(solution)/shard_map/all_to_all | solution.py:54
  335.8 96.7 %all-to-all-done.1 = bf16[32,12,2048]{2,1,0:T(8,128)(2,1)} async-done(((bf16[32,12,2048]{2,1,0:T(8,128)(2,1)}), bf16[32,12,2048]{2,1,0:T(8,128)(2,1)}, u32[]{:S(2)}, u32[]{:S(2)}) %all-to-all-start.1) | async-done | bytes 1572896 | tf_op jit(solution)/shard_map/all_to_all | solution.py:54
  432.5 2.5 copy.47
  434.9 4.3 gather_fusion
  439.2 1.3 reshape.110
  440.6 4.0 multiply_reduce_fusion
  (32 shorter events, 4.3 us)
Async XLA Ops:
  6.5 216.4 %all-gather.3.cloned.1.call-start = ((), (), s32[]{:S(2)}) async-start(), calls=%async_computation.2 | async-start | bytes 6684672 | tf_op jit(solution)/shard_map/all_gather | solution.py:37
  36.4 16.4 %copy-start.1 = (s32[16]{0:T(128)S(1)}, s32[16]{0:T(128)}, u32[]{:S(2)}) copy-start(s32[16]{0:T(128)} %param.13) | copy-start | bytes 196
  36.4 179.6 %all-to-all-start = ((bf16[32,12,2048]{2,1,0:T(8,128)(2,1)}), bf16[32,12,2048]{2,1,0:T(8,128)(2,1)}, u32[]{:S(2)}, u32[]{:S(2)}) async-start(bf16[32,12,2048]{2,1,0:T(8,128)(2,1)} %copy.40), calls=%async_computation | async-start | bytes 4194304 | tf_op jit(solution)/shard_map/all_to_all | solution.py:40
  52.0 261.1 %all-gather.5.cloned.1.call-start = ((), (), s32[]{:S(2)}) async-start(), calls=%async_computation.3 | async-start | bytes 3342336 | tf_op jit(solution)/shard_map/all_gather | solution.py:38
  321.5 14.1 %copy-start = (f32[128,2]{0,1:T(2,128)S(1)}, f32[128,2]{0,1:T(2,128)}, u32[]{:S(2)}) copy-start(f32[128,2]{0,1:T(2,128)} %param.10) | copy-start | bytes 3076
  321.5 110.9 %all-to-all-start.1 = ((bf16[32,12,2048]{2,1,0:T(8,128)(2,1)}), bf16[32,12,2048]{2,1,0:T(8,128)(2,1)}, u32[]{:S(2)}, u32[]{:S(2)}) async-start(bf16[32,12,2048]{2,1,0:T(8,128)(2,1)} %reshape.165), calls=%async_computation.1 | async-start | bytes 4194304 | tf_op jit(solution)/shard_map/all_to_all | solution.py:54
Sparse Core Ops, SparseCore 0:
  10.7 106.4 all-gather.2
  120.4 192.6 all-gather.4
where the time goes:
time: 452 us; the launch traced here: 451 us
  waiting for transfers between devices  344 us (76%)
  local copies, waits for them, and re-layouts  48.2 us (11%)
  starting transfers between devices  29.8 us (7%)
  between operations  13.7 us (3%)
  matrix products  10.8 us (2%)
  other arithmetic  5.24 us (1%)
    all_to_all x1, waiting for transfers between devices, local(): lax.all_to_all(outgoing, 'exp', split_axis=0, concat_axis=0, tiled=True)  162 us
    all_to_all x1, waiting for transfers between devices, local(): lax.all_to_all(produced.reshape(experts, slot_count, model_width), 'exp',...  96.7 us
    all_gather x1, waiting for transfers between devices, local(): lax.all_gather(down_store, 'rep', axis=2, tiled=True)  83.4 us
    scatter x2, local copies, waits for them, and re-layouts, local(): outgoing = jnp.zeros((experts, capacity, model_width), jnp.bfloat16).at[f...  24.7 us
    all_to_all x1, starting transfers between devices, local(): lax.all_to_all(outgoing, 'exp', split_axis=0, concat_axis=0, tiled=True)  15.6 us
    all_to_all x1, starting transfers between devices, local(): lax.all_to_all(produced.reshape(experts, slot_count, model_width), 'exp',...  14.1 us
  transfers between devices with their start and end apart: 4, of which 3 were waited for; matrix products, arithmetic and copies ran while one was open for 10% of the time, Pallas kernels for 0%

commit v1 on v0

v1 whole, which is shorter than its diff:
```python
import functools

import jax
import jax.numpy as jnp
from jax import lax
from jax.experimental import pallas as pl
from jax.experimental.pallas import tpu as pltpu
from jax.sharding import PartitionSpec as P

MESH = pl.DeviceIdType.MESH
D = 2048
H = 768
TOK = 128
DB = 128
NR = 16
PK = 16
PW = 1536
SLOTS = 32
ROWS = SLOTS * PK
STEPS = (4, 3, -3, 2, -2, 1, -1, 0)
GROUPS = ((0, 12), (12, 20), (20, 32))
SELF = 28
CH = 3
BF = jnp.bfloat16
F32 = jnp.float32


def dot(a, b):
    return jnp.dot(a, b, preferred_element_type=F32)


def kernel(
    held, tok, routes, weight, gu, dn, out,
    gu_all, dn_all, tperm, opk, rcv, ppk, ret, wmix, xbuf, hid, p3, phi,
    loc, zs, zr, xs, xr, cs, cr, ds, dr, rs, rr,
):
    rep = lax.axis_index("rep")
    ex = lax.axis_index("exp")
    c = rep % 2
    x = (rep // 2) % 4
    zh = rep // 8
    y = ex // 8
    z = zh * 8 + ex % 8

    def dev(ax, ay, az, ac):
        ax = (ax + 4) % 4
        ay = (ay + 4) % 4
        az = (az + 16) % 16
        return (((az // 8) * 4 + ax) * 2 + ac, ay * 8 + az % 8)

    def owner(azh, ax, ac):
        return (azh * 4 + (ax + 4) % 4) * 2 + ac

    def disp(k):
        return 4 - 8 * c if STEPS[k] == 4 else STEPS[k]

    partners = [dev(x, y, z + 8, c), dev(x, y, z, 1 - c)]
    partners += [dev(x + k, y, z, c) for k in (1, 2, 3)]
    for d in range(-4, 5):
        for dy in range(4):
            if d or dy:
                partners.append(dev(x, y + dy, z + d, c))
    barrier = pltpu.get_barrier_semaphore()
    for p in partners:
        pl.semaphore_signal(barrier, inc=1, device_id=p, device_id_type=MESH)
    pl.semaphore_wait(barrier, len(partners))

    mine = owner(zh, x, c)
    far = owner(1 - zh, x, c)

    def own(ch):
        return dn if ch == 2 else gu.at[pl.ds(64 * ch, 64)]

    def slot(r, ch):
        if ch == 2:
            return dn_all.at[r]
        return gu_all.at[pl.ds(pl.multiple_of(r * DB + 64 * ch, 64), 64)]

    def send(src, dst, ss, rsem, to):
        return pltpu.make_async_remote_copy(
            src_ref=src, dst_ref=dst, send_sem=ss, recv_sem=rsem,
            device_id=to, device_id_type=MESH,
        )

    started = []

    def go(cp):
        cp.start()
        started.append(cp)

    def arrived(dst, ss, rsem, to):
        send(dst, dst, ss, rsem, to).wait_recv()

    core = dev(x, y, z, 1 - c)
    for ch in range(CH):
        go(send(own(ch), slot(mine, ch), zs.at[ch], zr.at[ch], dev(x, y, z + 8, c)))
    for ch in range(CH):
        for k in (1, 3, 2):
            i = ch * 3 + k - 1
            go(send(own(ch), slot(mine, ch), xs.at[i], xr.at[i], dev(x + k, y, z, c)))
    for ch in range(CH):
        go(send(own(ch), slot(mine, ch), cs.at[ch], cr.at[ch], core))
    keep = [pltpu.make_async_copy(own(ch), slot(mine, ch), loc.at[ch]) for ch in range(CH)]
    for cp in keep:
        cp.start()

    for r in range(NR):
        pick = tok[:, 0:DB]
        for b in range(1, NR):
            pick = jnp.where(held[r] == b, tok[:, b * DB : (b + 1) * DB], pick)
        tperm[:, r * DB : (r + 1) * DB] = pick

    lane = lax.broadcasted_iota(jnp.int32, (TOK, 128), 1)
    row = lax.broadcasted_iota(jnp.int32, (TOK, 128), 0)
    lower = (lane < row).astype(F32).astype(BF)

    def column(v):
        return jnp.transpose(jnp.broadcast_to(v, (128, TOK)))

    named = [column(routes[k : k + 1, :].astype(F32)) for k in range(2)]
    share = [column(weight[k : k + 1, :]) for k in range(2)]
    hot0 = (lane.astype(F32) == named[0]).astype(F32)
    hot1 = (lane.astype(F32) == named[1]).astype(F32)
    seen0 = dot(lower, hot0.astype(BF))
    seen1 = dot(lower, hot1.astype(BF)) + jnp.sum(hot0, axis=0, keepdims=True)
    lanef = lane.astype(F32)
    wide = lax.broadcasted_iota(jnp.int32, (TOK, ROWS), 1).astype(F32)
    tall = row.astype(F32)
    keys = []
    for hot, seen in ((hot0, seen0), (hot1, seen1)):
        base = jnp.sum(hot * lanef, axis=1, keepdims=True) * PK
        rank = jnp.sum(hot * seen, axis=1, keepdims=True)
        quad = (rank >= 4.0).astype(F32) + (rank >= 8.0).astype(F32)
        keys.append((base + rank, base + 12.0 + rank - 4.0 * quad, quad))
    for j in range(4):
        mix = jnp.zeros((TOK, ROWS), F32)
        for k, (lo, hi, quad) in enumerate(keys):
            key = lo if j == 3 else jnp.where(quad == float(j), hi, -1.0)
            mix = mix + jnp.where(wide == key, share[k][:, 0:1], 0.0)
        top = mix.astype(BF)
        wmix[j, 0:TOK, :] = top
        wmix[j, TOK : 2 * TOK, :] = (mix - top.astype(F32)).astype(BF)
    turned = []
    for lo, hi, quad in keys:
        turned.append(
            tuple(jnp.transpose(jnp.broadcast_to(v, (TOK, 128))) for v in (lo, hi, quad))
        )
    for b in range(ROWS // 128):
        at = tall + float(b * 128)
        low = jnp.zeros((128, TOK), F32)
        for lo, hi, quad in turned:
            low = low + (at == lo).astype(F32)
        for j in range(3):
            high = jnp.zeros((128, TOK), F32)
            for lo, hi, quad in turned:
                high = high + (at == jnp.where(quad == float(j), hi, -1.0)).astype(F32)
            block = dot(low.astype(BF), tperm[:, 512 * j : 512 * (j + 1)])
            block = block + dot(high.astype(BF), tperm[:, PW:D])
            opk[b * 128 : (b + 1) * 128, 512 * j : 512 * (j + 1)] = block.astype(BF)

    def expert(k, dy):
        return ((y + dy) % 4) * 8 + (z + disp(k) + 16) % 8

    def tile(ref, e):
        return ref.at[pl.ds(pl.multiple_of(e * PK, PK), PK)]

    def dispatch(first, last):
        for i in range(first, last):
            if i == SELF:
                continue
            k, dy = i // 4, i % 4
            go(send(
                tile(opk, expert(k, dy)), tile(rcv, i), ds.at[i], dr.at[i],
                dev(x, y + dy, z + disp(k), c),
            ))

    def from_x(ch, part):
        for k in (1, 3, 2):
            i = part * 9 + ch * 3 + k - 1
            r = owner(zh if part == 0 else 1 - zh, x - k, c)
            arrived(slot(r, ch), xs.at[i], xr.at[i], dev(x + k, y, z, c))
            n = 6 + i
            go(send(slot(r, ch), slot(r, ch), cs.at[n], cr.at[n], core))

    for ch in range(CH):
        from_x(ch, 0)
        arrived(slot(far, ch), zs.at[ch], zr.at[ch], dev(x, y, z + 8, c))
        for k in (1, 3, 2):
            i = 9 + ch * 3 + k - 1
            go(send(slot(far, ch), slot(far, ch), xs.at[i], xr.at[i], dev(x + k, y, z, c)))
        go(send(slot(far, ch), slot(far, ch), cs.at[3 + ch], cr.at[3 + ch], core))
        if ch == 1:
            dispatch(0, SLOTS)
            rcv[SELF * PK : (SELF + 1) * PK, :] = opk[pl.ds(pl.multiple_of(ex * PK, PK), PK), :]
    for ch in range(CH):
        from_x(ch, 1)
    for ch in range(CH):
        arrived(slot(owner(zh, x, 1 - c), ch), cs.at[ch], cr.at[ch], core)
        arrived(slot(owner(1 - zh, x, 1 - c), ch), cs.at[3 + ch], cr.at[3 + ch], core)
        for part in range(2):
            for k in (1, 2, 3):
                n = 6 + part * 9 + ch * 3 + k - 1
                r = owner(zh if part == 0 else 1 - zh, x - k, 1 - c)
                arrived(slot(r, ch), cs.at[n], cr.at[n], core)
    for cp in keep:
        cp.wait()

    for first, last in GROUPS:
        n = (last - first) * PK
        lo = first * PK
        for i in range(first, last):
            if i == SELF:
                continue
            k, dy = i // 4, i % 4
            arrived(tile(rcv, i), ds.at[i], dr.at[i], dev(x, y + dy, z + disp(k), c))
        a = lax.broadcasted_iota(jnp.int32, (n, n), 0)
        b = lax.broadcasted_iota(jnp.int32, (n, n), 1)
        same = (a // PK) == (b // PK)
        ai, bi = a % PK, b % PK
        xbuf[0:n, 0:PW] = rcv[lo : lo + n, :]
        tail = jnp.zeros((n, 512), F32)
        for j in range(3):
            take = same & (ai // 4 == j) & (bi == 12 + ai % 4)
            tail = tail + dot(
                take.astype(F32).astype(BF), rcv[lo : lo + n, 512 * j : 512 * (j + 1)]
            )
        xbuf[0:n, PW:D] = tail.astype(BF)

        def up(t, carry):
            col = pl.multiple_of(t * 256, 256)
            g = dot(xbuf[0:n, :], gu_all[:, pl.ds(col, 256)])
            u = dot(xbuf[0:n, :], gu_all[:, pl.ds(pl.multiple_of(H + col, 256), 256)])
            hid[0:n, pl.ds(col, 256)] = (g / (1.0 + jnp.exp(-g)) * u).astype(BF)
            return carry

        lax.fori_loop(0, 3, up, 0)

        def down(q):
            w = jnp.concatenate([dn_all[2 * q], dn_all[2 * q + 1]], axis=1)
            return dot(hid[0:n, :], w).astype(BF)

        for q in (6, 7):
            p3[0:n, (q - 6) * 256 : (q - 5) * 256] = down(q)
        for j in range(3):
            put = same & (bi // 4 == j) & (ai == 12 + bi % 4)
            phi[0:n, 512 * j : 512 * (j + 1)] = dot(
                put.astype(F32).astype(BF), p3[0:n, :]
            ).astype(BF)
        real = lax.broadcasted_iota(jnp.int32, (n, 256), 0) % PK < 12

        def pack(q, carry):
            col = pl.multiple_of(q * 256, 256)
            v = jnp.where(real, down(q).astype(F32), phi[0:n, pl.ds(col, 256)].astype(F32))
            ppk[lo : lo + n, pl.ds(col, 256)] = v.astype(BF)
            return carry

        lax.fori_loop(0, 6, pack, 0)
        for i in range(first, last):
            if i == SELF:
                continue
            k, dy = i // 4, i % 4
            go(send(
                tile(ppk, i), tile(ret, ex), rs.at[i], rr.at[i],
                dev(x, y - dy, z - disp(k), c),
            ))
    ret[pl.ds(pl.multiple_of(ex * PK, PK), PK), :] = ppk[SELF * PK : (SELF + 1) * PK, :]

    for i in range(SLOTS):
        if i == SELF:
            continue
        k, dy = i // 4, i % 4
        arrived(tile(ret, expert(k, dy)), rs.at[i], rr.at[i], dev(x, y - dy, z - disp(k), c))

    last = jnp.zeros((2 * TOK, 512), F32)
    for j in range(3):
        block = ret[:, 512 * j : 512 * (j + 1)]
        m = dot(wmix[3], block)
        out[:, 512 * j : 512 * (j + 1)] = (m[0:TOK] + m[TOK : 2 * TOK]).astype(BF)
        last = last + dot(wmix[j], block)
    out[:, PW:D] = (last[0:TOK] + last[TOK : 2 * TOK]).astype(BF)

    for cp in started:
        cp.wait_send()


def restore(held, mixed, out):
    for r in range(NR):
        col = pl.multiple_of(held[r] * DB, DB)
        out[:, pl.ds(col, DB)] = mixed[:, r * DB : (r + 1) * DB]


def local(tokens, routes, route_weight, gate_up_store, down_store, held_bucket):
    vmem = pl.BlockSpec(memory_space=pltpu.VMEM)
    dma = pltpu.SemaphoreType.DMA
    most = max(b - a for a, b in GROUPS) * PK
    mixed = pl.pallas_call(
        kernel,
        out_shape=jax.ShapeDtypeStruct((TOK, D), BF),
        in_specs=[pl.BlockSpec(memory_space=pltpu.SMEM)] + [vmem] * 5,
        out_specs=vmem,
        scratch_shapes=[
            pltpu.VMEM((D, 2 * H), BF),
            pltpu.VMEM((NR, H, DB), BF),
            pltpu.VMEM((TOK, D), BF),
            pltpu.VMEM((ROWS, PW), BF),
            pltpu.VMEM((ROWS, PW), BF),
            pltpu.VMEM((ROWS, PW), BF),
            pltpu.VMEM((ROWS, PW), BF),
            pltpu.VMEM((4, 2 * TOK, ROWS), BF),
            pltpu.VMEM((most, D), BF),
            pltpu.VMEM((most, H), BF),
            pltpu.VMEM((most, 512), BF),
            pltpu.VMEM((most, PW), BF),
            dma((CH,)),
            dma((CH,)), dma((CH,)),
            dma((18,)), dma((18,)),
            dma((24,)), dma((24,)),
            dma((SLOTS,)), dma((SLOTS,)),
            dma((SLOTS,)), dma((SLOTS,)),
        ],
        compiler_params=pltpu.CompilerParams(
            collective_id=0, has_side_effects=True, vmem_limit_bytes=56 << 20
        ),
        name="layer",
    )(
        held_bucket, tokens, routes.T, route_weight.T,
        gate_up_store.reshape(DB, 2 * H), down_store.reshape(H, DB),
    )
    return pl.pallas_call(
        restore,
        out_shape=jax.ShapeDtypeStruct((TOK, D), BF),
        in_specs=[pl.BlockSpec(memory_space=pltpu.SMEM), vmem],
        out_specs=vmem,
        name="restore",
    )(held_bucket, mixed)


def solution(mesh):
    in_specs = (
        P(("rep", "exp"), None),
        P(("rep", "exp"), None),
        P(("rep", "exp"), None),
        P("exp", "rep", None),
        P("exp", None, "rep"),
        P(),
    )
    out_specs = P(("rep", "exp"), None)
    return jax.shard_map(local, mesh=mesh, in_specs=in_specs, out_specs=out_specs, check_vma=False)
```

time: 452 us -> 145 us (0.32)
  the two profiles are of different devices: /device:TPU:32 before, /device:TPU:36 now
where the time goes in v1:
time: 145 us
  Pallas kernels  145 us (100%)
    pallas_call x1, Pallas kernels, local(): pl.pallas_call(kernel, out_shape=jax.ShapeDtypeStruct((TOK, D), BF), in_s...  143 us

profile of v1, /device:TPU:36, one launch (start us, length us, event | category | flops | bytes accessed | tf_op | source)
XLA Modules:
  0.0 145.3 jit_solution(18240521634763311957)
XLA Ops:
  0.0 143.3 %layer.1.mixed = bf16[128,2048]{1,0:T(8,128)(2,1)} custom-call(s32[16]{0:T(128)} %held.3, bf16[128,2048]{1,0:T(8,128)(2,1)} %tok.1, s32[2,128]{1,0:T(2,128)} %bitcast.6, f32[2,128]{1,0:T(2,128)} %bitcast.7, bf16[128,1536]{1,0:T(8,128)(2,1)} %bitcast.4, bf16[768,128]{1,0:T(8,128)(2,1)} %bitcast.5), custom_call_target="tpu_custom_call" | custom-call | tf_op jit(solution)/shard_map/layer/pallas_call | solution.py:296
  143.3 2.0 %restore.1 = bf16[128,2048]{1,0:T(8,128)(2,1)} custom-call(s32[16]{0:T(128)} %held.3, bf16[128,2048]{1,0:T(8,128)(2,1)} %layer.1.mixed), custom_call_target="tpu_custom_call" | custom-call | tf_op jit(solution)/shard_map/restore/pallas_call | solution.py:329

commit v2 on v1

--- a/solution.py
+++ b/solution.py
@@ -19,6 +19,7 @@
 ROWS = SLOTS * PK
 STEPS = (4, 3, -3, 2, -2, 1, -1, 0)
 GROUPS = ((0, 12), (12, 20), (20, 32))
+MIX = ((0, 16), (16, 32))
 SELF = 28
 CH = 3
 BF = jnp.bfloat16
@@ -31,7 +32,7 @@
 
 def kernel(
     held, tok, routes, weight, gu, dn, out,
-    gu_all, dn_all, tperm, opk, rcv, ppk, ret, wmix, xbuf, hid, p3, phi,
+    gu_all, dn_all, tperm, opk, rcv, ppk, ret, wmix, xbuf, hid, p3, phi, comb,
     loc, zs, zr, xs, xr, cs, cr, ds, dr, rs, rr,
 ):
     rep = lax.axis_index("rep")
@@ -123,12 +124,14 @@
     hot1 = (lane.astype(F32) == named[1]).astype(F32)
     seen0 = dot(lower, hot0.astype(BF))
     seen1 = dot(lower, hot1.astype(BF)) + jnp.sum(hot0, axis=0, keepdims=True)
-    lanef = lane.astype(F32)
+    dz = (lane % 8 - ex % 8 + 8) % 8
+    step = jnp.where(dz < 4, 7 - 2 * dz, 2 * dz - 8)
+    place = (step * 4 + (lane // 8 - y + 16) % 4).astype(F32)
     wide = lax.broadcasted_iota(jnp.int32, (TOK, ROWS), 1).astype(F32)
     tall = row.astype(F32)
     keys = []
     for hot, seen in ((hot0, seen0), (hot1, seen1)):
-        base = jnp.sum(hot * lanef, axis=1, keepdims=True) * PK
+        base = jnp.sum(hot * place, axis=1, keepdims=True) * PK
         rank = jnp.sum(hot * seen, axis=1, keepdims=True)
         quad = (rank >= 4.0).astype(F32) + (rank >= 8.0).astype(F32)
         keys.append((base + rank, base + 12.0 + rank - 4.0 * quad, quad))
@@ -158,11 +161,8 @@
             block = block + dot(high.astype(BF), tperm[:, PW:D])
             opk[b * 128 : (b + 1) * 128, 512 * j : 512 * (j + 1)] = block.astype(BF)
 
-    def expert(k, dy):
-        return ((y + dy) % 4) * 8 + (z + disp(k) + 16) % 8
-
-    def tile(ref, e):
-        return ref.at[pl.ds(pl.multiple_of(e * PK, PK), PK)]
+    def tile(ref, i):
+        return ref.at[pl.ds(i * PK, PK)]
 
     def dispatch(first, last):
         for i in range(first, last):
@@ -170,7 +170,7 @@
                 continue
             k, dy = i // 4, i % 4
             go(send(
-                tile(opk, expert(k, dy)), tile(rcv, i), ds.at[i], dr.at[i],
+                tile(opk, i), tile(rcv, i), ds.at[i], dr.at[i],
                 dev(x, y + dy, z + disp(k), c),
             ))
 
@@ -191,7 +191,7 @@
         go(send(slot(far, ch), slot(far, ch), cs.at[3 + ch], cr.at[3 + ch], core))
         if ch == 1:
             dispatch(0, SLOTS)
-            rcv[SELF * PK : (SELF + 1) * PK, :] = opk[pl.ds(pl.multiple_of(ex * PK, PK), PK), :]
+            rcv[SELF * PK : (SELF + 1) * PK, :] = opk[SELF * PK : (SELF + 1) * PK, :]
     for ch in range(CH):
         from_x(ch, 1)
     for ch in range(CH):
@@ -260,24 +260,32 @@
                 continue
             k, dy = i // 4, i % 4
             go(send(
-                tile(ppk, i), tile(ret, ex), rs.at[i], rr.at[i],
+                tile(ppk, i), tile(ret, i), rs.at[i], rr.at[i],
                 dev(x, y - dy, z - disp(k), c),
             ))
-    ret[pl.ds(pl.multiple_of(ex * PK, PK), PK), :] = ppk[SELF * PK : (SELF + 1) * PK, :]
-
-    for i in range(SLOTS):
-        if i == SELF:
-            continue
-        k, dy = i // 4, i % 4
-        arrived(tile(ret, expert(k, dy)), rs.at[i], rr.at[i], dev(x, y - dy, z - disp(k), c))
-
-    last = jnp.zeros((2 * TOK, 512), F32)
-    for j in range(3):
-        block = ret[:, 512 * j : 512 * (j + 1)]
-        m = dot(wmix[3], block)
-        out[:, 512 * j : 512 * (j + 1)] = (m[0:TOK] + m[TOK : 2 * TOK]).astype(BF)
-        last = last + dot(wmix[j], block)
-    out[:, PW:D] = (last[0:TOK] + last[TOK : 2 * TOK]).astype(BF)
+    ret[SELF * PK : (SELF + 1) * PK, :] = ppk[SELF * PK : (SELF + 1) * PK, :]
+
+    def put(first, cols, m):
+        v = m[0:TOK] + m[TOK : 2 * TOK]
+        if first == 0:
+            comb[:, cols] = v
+        else:
+            out[:, cols] = (comb[:, cols] + v).astype(BF)
+
+    for first, last in MIX:
+        for i in range(first, last):
+            if i == SELF:
+                continue
+            k, dy = i // 4, i % 4
+            arrived(tile(ret, i), rs.at[i], rr.at[i], dev(x, y - dy, z - disp(k), c))
+        lo, hi = first * PK, last * PK
+        part = jnp.zeros((2 * TOK, 512), F32)
+        for j in range(3):
+            block = ret[lo:hi, 512 * j : 512 * (j + 1)]
+            m = dot(wmix[3, :, lo:hi], block)
+            part = part + dot(wmix[j, :, lo:hi], block)
+            put(first, slice(512 * j, 512 * (j + 1)), m)
+        put(first, slice(PW, D), part)
 
     for cp in started:
         cp.wait_send()
@@ -311,6 +319,7 @@
             pltpu.VMEM((most, H), BF),
             pltpu.VMEM((most, 512), BF),
             pltpu.VMEM((most, PW), BF),
+            pltpu.VMEM((TOK, D), F32),
             dma((CH,)),
             dma((CH,)), dma((CH,)),
             dma((18,)), dma((18,)),
@@ -319,7 +328,7 @@
             dma((SLOTS,)), dma((SLOTS,)),
         ],
         compiler_params=pltpu.CompilerParams(
-            collective_id=0, has_side_effects=True, vmem_limit_bytes=56 << 20
+            collective_id=0, has_side_effects=True, vmem_limit_bytes=28 << 20
         ),
         name="layer",
     )(
@@ -331,6 +340,7 @@
         out_shape=jax.ShapeDtypeStruct((TOK, D), BF),
         in_specs=[pl.BlockSpec(memory_space=pltpu.SMEM), vmem],
         out_specs=vmem,
+        compiler_params=pltpu.CompilerParams(vmem_limit_bytes=4 << 20),
         name="restore",
     )(held_bucket, mixed)
 

time: 145 us -> 147 us (1.014)
  the two profiles are of different devices: /device:TPU:36 before, /device:TPU:32 now
where the time goes in v2:
time: 147 us
  Pallas kernels  143 us (97%)
  local copies, waits for them, and re-layouts  3.67 us (2%)
    pallas_call x1, Pallas kernels, local(): pl.pallas_call(kernel, out_shape=jax.ShapeDtypeStruct((TOK, D), BF), in_s...  141 us
    unnamed x12, local copies, waits for them, and re-layouts  3.67 us

profile of v2, /device:TPU:32, one launch (start us, length us, event | category | flops | bytes accessed | tf_op | source)
XLA Modules:
  0.0 146.5 jit_solution(17089222921435451663)
XLA Ops:
  0.0 0.0 copy-start.5
  0.0 0.0 copy-start.3
  0.0 0.0 copy-start.4
  0.0 0.7 copy-done.5
  0.7 0.0 copy-done.3
  0.7 0.0 copy-done.4
  0.7 0.0 copy-start
  0.7 1.0 copy-done
  1.8 0.0 copy-start.1
  1.8 1.0 copy-done.1
  2.8 0.0 copy-start.2
  2.8 0.9 copy-done.2
  3.7 141.4 %layer.1.mixed = bf16[128,2048]{1,0:T(8,128)(2,1)S(1)} custom-call(s32[16]{0:T(128)S(1)} %copy-done.3, bf16[128,2048]{1,0:T(8,128)(2,1)S(1)} %copy-done, s32[2,128]{1,0:T(2,128)S(1)} %bitcast.6, f32[2,128]{1,0:T(2,128)S(1)} %bitcast.7, bf16[128,1536]{1,0:T(8,128)(2,1)S(1)} %bitcast.4, bf16[768,128]{1,0:T(8,128)(2,1)S(1)} %bitcast.5), custom_call_target="tpu_custom_call" | custom-call | tf_op jit(solution)/shard_map/layer/pallas_call | solution.py:304
  145.1 1.5 %restore.1 = bf16[128,2048]{1,0:T(8,128)(2,1)} custom-call(s32[16]{0:T(128)S(1)} %copy-done.3, bf16[128,2048]{1,0:T(8,128)(2,1)S(1)} %layer.1.mixed), custom_call_target="tpu_custom_call" | custom-call | tf_op jit(solution)/shard_map/restore/pallas_call | solution.py:338
Async XLA Ops:
  0.0 0.7 copy-start.5
  0.0 0.7 copy-start.3
  0.0 0.7 copy-start.4
  0.7 1.0 copy-start
  1.8 1.0 copy-start.1
  2.8 0.9 copy-start.2

commit v3 on v2

--- a/solution.py
+++ b/solution.py
@@ -31,9 +31,9 @@
 
 
 def kernel(
-    held, tok, routes, weight, gu, dn, out,
+    held, tok_in, routes_in, weight_in, gu, dn, out,
     gu_all, dn_all, tperm, opk, rcv, ppk, ret, wmix, xbuf, hid, p3, phi, comb,
-    loc, zs, zr, xs, xr, cs, cr, ds, dr, rs, rr,
+    tok, routes, weight, inp, loc, zs, zr, xs, xr, cs, cr, ds, dr, rs, rr,
 ):
     rep = lax.axis_index("rep")
     ex = lax.axis_index("exp")
@@ -54,6 +54,13 @@
 
     def disp(k):
         return 4 - 8 * c if STEPS[k] == 4 else STEPS[k]
+
+    loads = [
+        pltpu.make_async_copy(a, b, inp.at[i])
+        for i, (a, b) in enumerate(((tok_in, tok), (routes_in, routes), (weight_in, weight)))
+    ]
+    for cp in loads:
+        cp.start()
 
     partners = [dev(x, y, z + 8, c), dev(x, y, z, 1 - c)]
     partners += [dev(x + k, y, z, c) for k in (1, 2, 3)]
@@ -104,6 +111,9 @@
     keep = [pltpu.make_async_copy(own(ch), slot(mine, ch), loc.at[ch]) for ch in range(CH)]
     for cp in keep:
         cp.start()
+
+    for cp in loads:
+        cp.wait()
 
     for r in range(NR):
         pick = tok[:, 0:DB]
@@ -304,7 +314,8 @@
     mixed = pl.pallas_call(
         kernel,
         out_shape=jax.ShapeDtypeStruct((TOK, D), BF),
-        in_specs=[pl.BlockSpec(memory_space=pltpu.SMEM)] + [vmem] * 5,
+        in_specs=[pl.BlockSpec(memory_space=pltpu.SMEM)]
+        + [pl.BlockSpec(memory_space=pltpu.HBM)] * 5,
         out_specs=vmem,
         scratch_shapes=[
             pltpu.VMEM((D, 2 * H), BF),
@@ -320,6 +331,10 @@
             pltpu.VMEM((most, 512), BF),
             pltpu.VMEM((most, PW), BF),
             pltpu.VMEM((TOK, D), F32),
+            pltpu.VMEM((TOK, D), BF),
+            pltpu.VMEM((2, TOK), jnp.int32),
+            pltpu.VMEM((2, TOK), F32),
+            dma((3,)),
             dma((CH,)),
             dma((CH,)), dma((CH,)),
             dma((18,)), dma((18,)),
@@ -328,7 +343,7 @@
             dma((SLOTS,)), dma((SLOTS,)),
         ],
         compiler_params=pltpu.CompilerParams(
-            collective_id=0, has_side_effects=True, vmem_limit_bytes=28 << 20
+            collective_id=0, has_side_effects=True, vmem_limit_bytes=60 << 20
         ),
         name="layer",
     )(
@@ -340,7 +355,6 @@
         out_shape=jax.ShapeDtypeStruct((TOK, D), BF),
         in_specs=[pl.BlockSpec(memory_space=pltpu.SMEM), vmem],
         out_specs=vmem,
-        compiler_params=pltpu.CompilerParams(vmem_limit_bytes=4 << 20),
         name="restore",
     )(held_bucket, mixed)
 

time: 147 us -> 145 us (0.986)
  the two profiles are of different devices: /device:TPU:32 before, /device:TPU:38 now
where the time goes in v3:
time: 145 us
  Pallas kernels  144 us (99%)
    pallas_call x1, Pallas kernels, local(): pl.pallas_call(kernel, out_shape=jax.ShapeDtypeStruct((TOK, D), BF), in_s...  143 us

profile of v3, /device:TPU:38, one launch (start us, length us, event | category | flops | bytes accessed | tf_op | source)
XLA Modules:
  0.0 144.5 jit_solution(17693826887451185274)
XLA Ops:
  0.0 142.5 %layer.1.mixed = bf16[128,2048]{1,0:T(8,128)(2,1)} custom-call(s32[16]{0:T(128)} %held.3, bf16[128,2048]{1,0:T(8,128)(2,1)} %tok_in.1, s32[2,128]{1,0:T(2,128)} %bitcast.6, f32[2,128]{1,0:T(2,128)} %bitcast.7, bf16[128,1536]{1,0:T(8,128)(2,1)} %bitcast.4, bf16[768,128]{1,0:T(8,128)(2,1)} %bitcast.5), custom_call_target="tpu_custom_call" | custom-call | tf_op jit(solution)/shard_map/layer/pallas_call | solution.py:314
  142.5 2.0 %restore.1 = bf16[128,2048]{1,0:T(8,128)(2,1)} custom-call(s32[16]{0:T(128)} %held.3, bf16[128,2048]{1,0:T(8,128)(2,1)} %layer.1.mixed), custom_call_target="tpu_custom_call" | custom-call | tf_op jit(solution)/shard_map/restore/pallas_call | solution.py:353

commit v4 on v3

--- a/solution.py
+++ b/solution.py
@@ -301,10 +301,16 @@
         cp.wait_send()
 
 
-def restore(held, mixed, out):
+def restore(held, mixed, out, sems):
+    copies = []
     for r in range(NR):
         col = pl.multiple_of(held[r] * DB, DB)
-        out[:, pl.ds(col, DB)] = mixed[:, r * DB : (r + 1) * DB]
+        copies.append(pltpu.make_async_copy(
+            mixed.at[:, pl.ds(r * DB, DB)], out.at[:, pl.ds(col, DB)], sems.at[r]
+        ))
+        copies[-1].start()
+    for cp in copies:
+        cp.wait()
 
 
 def local(tokens, routes, route_weight, gate_up_store, down_store, held_bucket):
@@ -353,8 +359,9 @@
     return pl.pallas_call(
         restore,
         out_shape=jax.ShapeDtypeStruct((TOK, D), BF),
-        in_specs=[pl.BlockSpec(memory_space=pltpu.SMEM), vmem],
-        out_specs=vmem,
+        in_specs=[pl.BlockSpec(memory_space=pltpu.SMEM), pl.BlockSpec(memory_space=pltpu.HBM)],
+        out_specs=pl.BlockSpec(memory_space=pltpu.HBM),
+        scratch_shapes=[dma((NR,))],
         name="restore",
     )(held_bucket, mixed)
 

time: 145 us -> 160 us (1.10)
  Pallas kernels: 144 us -> 160 us
    pallas_call x1, Pallas kernels: 1.97 us -> 17.8 us  [local(): pl.pallas_call(restore, out_shape=jax.ShapeDtypeStruct((TOK, D), BF), in_...]
where the time goes in v4:
time: 160 us
  Pallas kernels  160 us (100%)
    pallas_call x1, Pallas kernels, local(): pl.pallas_call(kernel, out_shape=jax.ShapeDtypeStruct((TOK, D), BF), in_s...  143 us
    pallas_call x1, Pallas kernels, local(): pl.pallas_call(restore, out_shape=jax.ShapeDtypeStruct((TOK, D), BF), in_...  17.8 us

profile of v4, /device:TPU:38, one launch (start us, length us, event | category | flops | bytes accessed | tf_op | source)
XLA Modules:
  0.0 160.3 jit_solution(15442280221720484048)
XLA Ops:
  0.0 142.5 %layer.1.mixed = bf16[128,2048]{1,0:T(8,128)(2,1)} custom-call(s32[16]{0:T(128)} %held.3, bf16[128,2048]{1,0:T(8,128)(2,1)} %tok_in.1, s32[2,128]{1,0:T(2,128)} %bitcast.6, f32[2,128]{1,0:T(2,128)} %bitcast.7, bf16[128,1536]{1,0:T(8,128)(2,1)} %bitcast.4, bf16[768,128]{1,0:T(8,128)(2,1)} %bitcast.5), custom_call_target="tpu_custom_call" | custom-call | tf_op jit(solution)/shard_map/layer/pallas_call | solution.py:320
  142.5 17.8 %restore.1 = bf16[128,2048]{1,0:T(8,128)(2,1)} custom-call(s32[16]{0:T(128)} %held.3, bf16[128,2048]{1,0:T(8,128)(2,1)} %layer.1.mixed), custom_call_target="tpu_custom_call" | custom-call | tf_op jit(solution)/shard_map/restore/pallas_call | solution.py:359

commit v5 on v4

--- a/solution.py
+++ b/solution.py
@@ -359,7 +359,7 @@
     return pl.pallas_call(
         restore,
         out_shape=jax.ShapeDtypeStruct((TOK, D), BF),
-        in_specs=[pl.BlockSpec(memory_space=pltpu.SMEM), pl.BlockSpec(memory_space=pltpu.HBM)],
+        in_specs=[pl.BlockSpec(memory_space=pltpu.SMEM), vmem],
         out_specs=pl.BlockSpec(memory_space=pltpu.HBM),
         scratch_shapes=[dma((NR,))],
         name="restore",

time: 160 us -> 145 us (0.906)
  Pallas kernels: 160 us -> 144 us
    pallas_call x1, Pallas kernels: 17.8 us -> 1.97 us  [local(): pl.pallas_call(restore, out_shape=jax.ShapeDtypeStruct((TOK, D), BF), in_...]
where the time goes in v5:
time: 145 us
  Pallas kernels  144 us (99%)
    pallas_call x1, Pallas kernels, local(): pl.pallas_call(kernel, out_shape=jax.ShapeDtypeStruct((TOK, D), BF), in_s...  143 us

profile of v5, /device:TPU:38, one launch (start us, length us, event | category | flops | bytes accessed | tf_op | source)
XLA Modules:
  0.0 144.5 jit_solution(16496755767997772752)
XLA Ops:
  0.0 142.5 %layer.1.mixed = bf16[128,2048]{1,0:T(8,128)(2,1)} custom-call(s32[16]{0:T(128)} %held.3, bf16[128,2048]{1,0:T(8,128)(2,1)} %tok_in.1, s32[2,128]{1,0:T(2,128)} %bitcast.6, f32[2,128]{1,0:T(2,128)} %bitcast.7, bf16[128,1536]{1,0:T(8,128)(2,1)} %bitcast.4, bf16[768,128]{1,0:T(8,128)(2,1)} %bitcast.5), custom_call_target="tpu_custom_call" | custom-call | tf_op jit(solution)/shard_map/layer/pallas_call | solution.py:320
  142.5 2.0 %restore.1 = bf16[128,2048]{1,0:T(8,128)(2,1)} custom-call(s32[16]{0:T(128)} %held.3, bf16[128,2048]{1,0:T(8,128)(2,1)} %layer.1.mixed), custom_call_target="tpu_custom_call" | custom-call | tf_op jit(solution)/shard_map/restore/pallas_call | solution.py:359
